TPU v7x, 256 devices: a whole 4x4x8 slice. The times are simulated.
256 devices in a mesh: row: 4 (over z_lo, core), col: 16 (over x, y), chan: 4 (over z_hi).
Axes of the slice: x: 4, y: 4, z: 8 (z_hi: 4, z_lo: 2; z = z_hi * 2 + z_lo), core: 2. Of those that a mesh axis runs over, the one named last changes fastest.
Arguments:
- pair: bfloat16 [1024, 1024, 128], P('row', 'col'), may hold values from -6 to 6
- pair_mask: int32 [1024, 1024], P('row', 'col'), may hold values 0 or 1
- ln_gain: float32 [128], replicated, may hold values from 0.1 to 1.9
- ln_bias: float32 [128], replicated, may hold values from -3 to 3
- left_value: bfloat16 [128, 128], P(None, 'chan'), may hold values from -0.5 to 0.5
- left_gate: bfloat16 [128, 128], P(None, 'chan'), may hold values from -0.5 to 0.5
- right_value: bfloat16 [128, 128], P(None, 'chan'), may hold values from -0.5 to 0.5
- right_gate: bfloat16 [128, 128], P(None, 'chan'), may hold values from -0.5 to 0.5
- hid_gain: float32 [128], replicated, may hold values from 0.1 to 1.9
- hid_bias: float32 [128], replicated, may hold values from -3 to 3
- out_weight: bfloat16 [128, 128], replicated, may hold values from -0.5 to 0.5
- out_gate: bfloat16 [128, 128], replicated, may hold values from -0.5 to 0.5
Outputs:
- update: bfloat16 [1024, 1024, 128], P('row', ('col', 'chan'))
All inputs are finite; a program needn't handle non-finite values. No bound on the sum of `pair_mask` on one device may be relied on, other than what follows from the above.
Results may differ from a plain program's by a relative error of at most 0.025.
Values may be sent and summed in bfloat16 or wider, within the bound.
No kernel may reach another device: no remote copies, remote signals or barrier semaphores. Data moves between devices by JAX's collectives and lax.ppermute only.
A program may use at most 128 MiB of HBM per device.

v0:
```python
import jax
import jax.numpy as jnp
from jax import lax
from jax.sharding import PartitionSpec as P


def on_device(
    pair,
    pair_mask,
    ln_gain,
    ln_bias,
    left_value,
    left_gate,
    right_value,
    right_gate,
    hid_gain,
    hid_bias,
    out_weight,
    out_gate,
):
    tile_cols = pair.shape[1]
    group_width = left_value.shape[1]
    out_cols = tile_cols // lax.axis_size("chan")
    group_index = lax.axis_index("chan")
    source = pair.astype(jnp.float32)
    centre = jnp.mean(source, axis=-1, keepdims=True)
    shifted = source - centre
    spread = jnp.mean(shifted * shifted, axis=-1, keepdims=True)
    normed = (shifted * lax.rsqrt(spread + 1e-05) * ln_gain + ln_bias).astype(jnp.bfloat16)
    weights = jnp.concatenate([left_value, left_gate, right_value, right_gate], axis=1)
    projected_all = jnp.einsum("ikc,cq->qik", normed, weights, preferred_element_type=jnp.float32)
    valid = pair_mask.astype(jnp.float32)[None, :, :]
    left = (
        jax.nn.sigmoid(projected_all[group_width : 2 * group_width])
        * projected_all[:group_width]
        * valid
    ).astype(jnp.bfloat16)
    right = (
        jax.nn.sigmoid(projected_all[3 * group_width :])
        * projected_all[2 * group_width : 3 * group_width]
        * valid
    ).astype(jnp.bfloat16)
    own_normed = lax.dynamic_slice_in_dim(normed, group_index * out_cols, out_cols, 1)
    gating = jax.nn.sigmoid(
        jnp.einsum("ijc,cd->ijd", own_normed, out_gate, preferred_element_type=jnp.float32)
    )
    right_all = lax.all_gather(right, "row", axis=1, tiled=True)
    product = lax.psum_scatter(
        jnp.einsum("hik,hjk->jhi", left, right_all, preferred_element_type=jnp.float32).astype(
            jnp.bfloat16
        ),
        "col",
        scatter_dimension=0,
        tiled=True,
    ).astype(jnp.float32)
    product = product.astype(jnp.bfloat16)
    widened = product.astype(jnp.float32)
    first_sums = jnp.sum(widened, axis=1)
    second_sums = jnp.sum(widened * widened, axis=1)
    first_sums, second_sums = (
        lax.psum(first_sums.astype(jnp.bfloat16), "chan").astype(jnp.float32),
        lax.psum(second_sums.astype(jnp.bfloat16), "chan").astype(jnp.float32),
    )
    total_width = group_width * lax.axis_size("chan")
    mean_hid = first_sums / total_width
    spread_hid = second_sums / total_width - mean_hid * mean_hid
    gain_part = lax.dynamic_slice_in_dim(hid_gain, group_index * group_width, group_width, 0)
    bias_part = lax.dynamic_slice_in_dim(hid_bias, group_index * group_width, group_width, 0)
    weight_rows = lax.dynamic_slice_in_dim(out_weight, group_index * group_width, group_width, 0)
    hidden = (
        (widened - mean_hid[:, None, :])
        * lax.rsqrt(spread_hid + 1e-05)[:, None, :]
        * gain_part[None, :, None]
        + bias_part[None, :, None]
    ).astype(jnp.bfloat16)
    mixed = lax.psum_scatter(
        jnp.einsum("jhi,hd->jid", hidden, weight_rows, preferred_element_type=jnp.float32).astype(
            jnp.bfloat16
        ),
        "chan",
        scatter_dimension=0,
        tiled=True,
    ).astype(jnp.float32)
    return (gating * jnp.transpose(mixed, (1, 0, 2))).astype(jnp.bfloat16)


def solution(mesh):
    return jax.shard_map(
        on_device,
        mesh=mesh,
        in_specs=(
            P("row", "col", None),
            P("row", "col"),
            P(),
            P(),
            P(None, "chan"),
            P(None, "chan"),
            P(None, "chan"),
            P(None, "chan"),
            P(),
            P(),
            P(),
            P(),
        ),
        out_specs=P("row", ("col", "chan"), None),
        check_vma=False,
    )
```

profile of v0, /device:TPU:1, one launch (start us, length us, event | category | flops | bytes accessed | tf_op | source)
XLA Modules:
  0.0 375.0 jit_solution(5184248092818221821)
XLA Ops:
  6.5 0.0 copy-start
  6.5 0.0 copy-start.3
  6.5 0.0 copy-start.9
  6.5 0.0 copy-start.8
  6.5 0.0 all-gather.2.cloned.1.call-start
  6.6 0.0 copy-start.1
  6.6 10.7 %convert_reduce_fusion = f32[256,64]{0,1:T(8,128)S(1)} fusion(bf16[256,64,128]{2,1,0:T(8,128)(2,1)} %param.12), kind=kLoop, calls=%fused_computation.2 | loop fusion | flops 4177920 | bytes 4259840 | tf_op jit(solution)/shard_map/reduce_sum | solution.py:26
  17.3 0.0 copy-done.1
  17.3 11.6 %fusion.2 = f32[256,64]{0,1:T(8,128)S(1)} fusion(f32[256,64]{0,1:T(8,128)S(1)} %broadcast_multiply_fusion, bf16[256,64,128]{2,1,0:T(8,128)(2,1)S(1)} %copy-done.1), kind=kLoop, calls=%fused_computation.5 | loop fusion | flops 8372224 | bytes 4325376 | tf_op jit(solution)/shard_map/reduce_sum | solution.py:28
  29.0 0.0 copy-done.3
  29.0 0.0 copy-done.9
  29.0 0.0 copy-done.8
  29.0 0.0 copy-start.4
  29.0 0.0 copy-start.5
  29.0 0.0 copy-start.6
  29.1 0.0 copy-start.7
  29.1 9.3 %fusion.5 = bf16[256,64,128]{2,0,1:T(8,128)(2,1)S(1)} fusion(f32[128]{0:T(128)S(1)} %copy-done.8, f32[128]{0:T(128)S(1)} %copy-done.9, f32[256,64]{0,1:T(8,128)S(1)} %add_rsqrt_fusion.1, f32[256,64]{0,1:T(8,128)S(1)} %broadcast_multiply_fusion, bf16[256,64,128]{2,1,0:T(8,128)(2,1)S(1)} %copy-done.1), kind=kLoop, calls=%fused_computation.8 | loop fusion | flops 12582912 | bytes 8520704 | tf_op jit(solution)/shard_map/convert_element_type | solution.py:29
  38.4 0.0 copy-done.4
  38.4 0.0 copy-done.5
  38.4 0.0 copy-done.6
  38.4 0.0 copy-done.7
  38.4 0.0 copy-start.2
  38.4 1.3 fusion.26
  39.7 0.7 copy-done.2
  40.3 2.4 fusion.13
  42.7 0.0 all-gather.2.cloned.1.call-update
  42.8 0.0 reduce-scatter.3.cloned.1.call-start
  42.8 53.4 %all-gather.2.cloned.1.call-done = bf16[32,1024,64]{1,0,2:T(8,128)(2,1)} async-done(((bf16[32,256,64]{1,0,2:T(8,128)(2,1)}), bf16[32,1024,64]{1,0,2:T(8,128)(2,1)}) %all-gather.2.cloned.1.call-update) | async-done | bytes 4194320 | tf_op jit(solution)/shard_map/all_gather | solution.py:47
  96.2 10.3 %convert_bitcast_fusion = bf16[1024,32,256]{2,0,1:T(8,128)(2,1)} fusion(bf16[32,1024,64]{1,0,2:T(8,128)(2,1)} %all-gather.2.cloned.1.call-done, bf16[32,256,64]{1,0,2:T(8,128)(2,1)S(1)} %get-tuple-element.7), kind=kOutput, calls=%fused_computation | convolution fusion | flops 1082130432 | bytes 22020096 | tf_op jit(solution)/shard_map/hik,hjk->jhi/dot_general | solution.py:49
  106.5 0.0 copy-start.11
  106.5 0.0 copy-start.12
  106.5 0.0 reduce-scatter.3.cloned.1.call-update
  106.5 0.0 all-reduce.3.cloned.1.call-start
  106.6 115.2 %reduce-scatter.3.cloned.1.call-done = bf16[64,32,256]{2,0,1:T(8,128)(2,1)} async-done(((bf16[1024,32,256]{2,0,1:T(8,128)(2,1)}), bf16[64,32,256]{2,0,1:T(8,128)(2,1)}) %reduce-scatter.3.cloned.1.call-update) | async-done | bytes 1048592 | tf_op jit(solution)/shard_map/reduce_scatter | solution.py:48
  221.8 2.1 fusion.11
  223.8 2.0 reduce_sum.41
  225.8 0.0 all-reduce.3.cloned.1.call-update
  225.8 0.3 reduce-scatter.5.cloned.1.call-start
  226.1 0.0 copy-done.11
  226.1 0.1 dynamic_slice.13
  226.2 0.0 copy-done.12
  226.2 0.1 dynamic_slice.14
  226.3 47.2 %all-reduce.3.cloned.1.call-done = (bf16[64,256]{1,0:T(8,128)(2,1)}, bf16[64,256]{1,0:T(8,128)(2,1)}) async-done(((bf16[64,256]{1,0:T(8,128)(2,1)}, bf16[64,256]{1,0:T(8,128)(2,1)}), (bf16[64,256]{1,0:T(8,128)(2,1)}, bf16[64,256]{1,0:T(8,128)(2,1)})) %all-reduce.3.cloned.1.call-update) | async-done | bytes 65552 | tf_op jit(solution)/shard_map/psum | solution.py:62
  273.5 0.8 convert_multiply_fusion.1
  274.3 1.6 fusion.10
  275.9 0.0 copy-done
  275.9 0.0 copy-start.10
  275.9 3.3 convolution_convert_fusion
  279.2 0.0 reduce-scatter.5.cloned.1.call-update
  279.2 85.3 %reduce-scatter.5.cloned.1.call-done = bf16[16,256,128]{2,1,0:T(8,128)(2,1)} async-done(((bf16[64,256,128]{2,1,0:T(8,128)(2,1)}), bf16[16,256,128]{2,1,0:T(8,128)(2,1)}) %reduce-scatter.5.cloned.1.call-update) | async-done | bytes 1048592 | tf_op jit(solution)/shard_map/reduce_scatter | solution.py:76
  364.5 0.0 copy-done.10
  364.5 2.2 fusion.22
  366.8 1.6 copy.17
  (3 shorter events, 0.0 us)
Async XLA Ops:
  6.5 269.4 %copy-start = (bf16[128,128]{1,0:T(8,128)(2,1)S(1)}, bf16[128,128]{1,0:T(8,128)(2,1)}, u32[]{:S(2)}) copy-start(bf16[128,128]{1,0:T(8,128)(2,1)} %param.22) | copy-start | bytes 98308
  6.5 22.4 %copy-start.3 = (s32[256,64]{0,1:T(8,128)S(1)}, s32[256,64]{0,1:T(8,128)}, u32[]{:S(2)}) copy-start(s32[256,64]{0,1:T(8,128)} %param.13) | copy-start | bytes 196612
  6.5 22.5 %copy-start.9 = (f32[128]{0:T(128)S(1)}, f32[128]{0:T(128)}, u32[]{:S(2)}) copy-start(f32[128]{0:T(128)} %param.14) | copy-start | bytes 1540
  6.5 22.5 %copy-start.8 = (f32[128]{0:T(128)S(1)}, f32[128]{0:T(128)}, u32[]{:S(2)}) copy-start(f32[128]{0:T(128)} %param.15) | copy-start | bytes 1540
  6.5 89.7 %all-gather.2.cloned.1.call-start = ((), (), s32[]{:S(2)}) async-start(), calls=%async_computation.2 | async-start | bytes 5242880 | tf_op jit(solution)/shard_map/all_gather | solution.py:47
  6.6 10.7 %copy-start.1 = (bf16[256,64,128]{2,1,0:T(8,128)(2,1)S(1)}, bf16[256,64,128]{2,1,0:T(8,128)(2,1)}, u32[]{:S(2)}) copy-start(bf16[256,64,128]{2,1,0:T(8,128)(2,1)} %param.12) | copy-start | bytes 12582916
  29.0 9.3 %copy-start.4 = (bf16[128,32]{0,1:T(8,128)(2,1)S(1)}, bf16[128,32]{0,1:T(8,128)(2,1)}, u32[]{:S(2)}) copy-start(bf16[128,32]{0,1:T(8,128)(2,1)} %param.19) | copy-start | bytes 24580
  29.0 9.3 %copy-start.5 = (bf16[128,32]{0,1:T(8,128)(2,1)S(1)}, bf16[128,32]{0,1:T(8,128)(2,1)}, u32[]{:S(2)}) copy-start(bf16[128,32]{0,1:T(8,128)(2,1)} %param.18) | copy-start | bytes 24580
  29.0 9.3 %copy-start.6 = (bf16[128,32]{0,1:T(8,128)(2,1)S(1)}, bf16[128,32]{0,1:T(8,128)(2,1)}, u32[]{:S(2)}) copy-start(bf16[128,32]{0,1:T(8,128)(2,1)} %param.17) | copy-start | bytes 24580
  29.1 9.3 %copy-start.7 = (bf16[128,32]{0,1:T(8,128)(2,1)S(1)}, bf16[128,32]{0,1:T(8,128)(2,1)}, u32[]{:S(2)}) copy-start(bf16[128,32]{0,1:T(8,128)(2,1)} %param.16) | copy-start | bytes 24580
  38.4 1.9 copy-start.2
  42.8 179.0 %reduce-scatter.3.cloned.1.call-start = ((), (), s32[]{:S(2)}) async-start(), calls=%async_computation.3 | async-start | bytes 17825792 | tf_op jit(solution)/shard_map/reduce_scatter | solution.py:48
  106.5 119.6 %copy-start.11 = (f32[128]{0:T(128)S(1)}, f32[128]{0:T(128)}, u32[]{:S(2)}) copy-start(f32[128]{0:T(128)} %param.20) | copy-start | bytes 1540
  106.5 119.7 %copy-start.12 = (f32[128]{0:T(128)S(1)}, f32[128]{0:T(128)}, u32[]{:S(2)}) copy-start(f32[128]{0:T(128)} %param.21) | copy-start | bytes 1540
  106.5 167.0 %all-reduce.3.cloned.1.call-start = ((), (), s32[]{:S(2)}) async-start(), calls=%async_computation.5 | async-start | bytes 131072 | tf_op jit(solution)/shard_map/psum | solution.py:62
  225.8 138.7 %reduce-scatter.5.cloned.1.call-start = ((), (), s32[]{:S(2)}) async-start(), calls=%async_computation.4 | async-start | bytes 5242880 | tf_op jit(solution)/shard_map/reduce_scatter | solution.py:76
  275.9 88.6 %copy-start.10 = (bf16[128,128]{1,0:T(8,128)(2,1)S(1)}, bf16[128,128]{1,0:T(8,128)(2,1)}, u32[]{:S(2)}) copy-start(bf16[128,128]{1,0:T(8,128)(2,1)} %param.23) | copy-start | bytes 98308
Sparse Core Ops, SparseCore 0:
  42.9 53.2 all-gather.1
  106.6 115.0 reduce-scatter.2
  226.0 47.4 all-reduce.2
  279.4 85.1 reduce-scatter.4
where the time goes:
time: 375 us
  waiting for transfers between devices  301 us (80%)
  other arithmetic  40.5 us (11%)
  matrix products  17 us (5%)
  between operations  13.3 us (4%)
    reduce_scatter x1, waiting for transfers between devices, on_device(): lax.psum_scatter(jnp.einsum('hik,hjk->jhi', left, right_all, preferred_el...  115 us
    reduce_scatter x1, waiting for transfers between devices, on_device(): lax.psum_scatter(jnp.einsum('jhi,hd->jid', hidden, weight_rows, preferred...  85.3 us
    all_gather x1, waiting for transfers between devices, on_device(): right_all = lax.all_gather(right, 'row', axis=1, tiled=True)  53.4 us
    psum x1, waiting for transfers between devices, on_device(): lax.psum(second_sums.astype(jnp.bfloat16), 'chan').astype(jnp.float32)  47.2 us
    reduce_sum x1, other arithmetic, on_device(): spread = jnp.mean(shifted * shifted, axis=-1, keepdims=True)  11.6 us
    reduce_sum x1, other arithmetic, on_device(): centre = jnp.mean(source, axis=-1, keepdims=True)  10.7 us
    dot_general x1, matrix products, on_device(): jnp.einsum('hik,hjk->jhi', left, right_all, preferred_element_type=jnp.fl...  10.3 us
    convert_element_type x1, other arithmetic, on_device(): (shifted * lax.rsqrt(spread + 1e-05) * ln_gain + ln_bias).astype(jnp.bflo...  9.28 us
  transfers between devices with their start and end apart: 4, of which 4 were waited for; matrix products, arithmetic and copies ran while one was open for 0% of the time, Pallas kernels for 0%

commit v1 on v0

--- a/solution.py
+++ b/solution.py
@@ -44,7 +44,9 @@
     gating = jax.nn.sigmoid(
         jnp.einsum("ijc,cd->ijd", own_normed, out_gate, preferred_element_type=jnp.float32)
     )
-    right_all = lax.all_gather(right, "row", axis=1, tiled=True)
+    right_all = jnp.concatenate(
+        lax.all_to_all(jnp.stack([right] * lax.axis_size("row")), "row", 0, 0), axis=1
+    )
     product = lax.psum_scatter(
         jnp.einsum("hik,hjk->jhi", left, right_all, preferred_element_type=jnp.float32).astype(
             jnp.bfloat16

time: 375 us -> 375 us (level)
  blocking collectives: 0 us -> 52.9 us
  waiting for transfers between devices: 301 us -> 249 us
    all_gather x1 -> x0, waiting for transfers between devices: 53.4 us -> none  [on_device(): right_all = lax.all_gather(right, 'row', axis=1, tiled=True)]
    all_to_all x0 -> x1, blocking collectives: none -> 52.9 us  [on_device(): lax.all_to_all(jnp.stack([right] * lax.axis_size('row')), 'row', 0, 0)]
  transfers between devices with their start and end apart: 4 -> 3, of which waited for: 4 -> 3; matrix products, arithmetic and copies ran while one was open for 0% -> 0% of each run, Pallas kernels for 0% -> 0%
where the time goes in v1:
time: 375 us
  waiting for transfers between devices  249 us (66%)
  blocking collectives  52.9 us (14%)
  other arithmetic  39.6 us (11%)
  matrix products  14.9 us (4%)
  between operations  13.4 us (4%)
  local copies, waits for them, and re-layouts  4.14 us (1%)
    reduce_scatter x1, waiting for transfers between devices, on_device(): lax.psum_scatter(jnp.einsum('hik,hjk->jhi', left, right_all, preferred_el...  117 us
    reduce_scatter x1, waiting for transfers between devices, on_device(): lax.psum_scatter(jnp.einsum('jhi,hd->jid', hidden, weight_rows, preferred...  85.3 us
    all_to_all x1, blocking collectives, on_device(): lax.all_to_all(jnp.stack([right] * lax.axis_size('row')), 'row', 0, 0)  52.9 us
    psum x1, waiting for transfers between devices, on_device(): lax.psum(second_sums.astype(jnp.bfloat16), 'chan').astype(jnp.float32)  47.1 us
    reduce_sum x1, other arithmetic, on_device(): spread = jnp.mean(shifted * shifted, axis=-1, keepdims=True)  11.6 us
    reduce_sum x1, other arithmetic, on_device(): centre = jnp.mean(source, axis=-1, keepdims=True)  10.7 us
    convert_element_type x1, other arithmetic, on_device(): (shifted * lax.rsqrt(spread + 1e-05) * ln_gain + ln_bias).astype(jnp.bflo...  9.28 us
    dot_general x1, matrix products, on_device(): jnp.einsum('hik,hjk->jhi', left, right_all, preferred_element_type=jnp.fl...  8.16 us
  transfers between devices with their start and end apart: 3, of which 3 were waited for; matrix products, arithmetic and copies ran while one was open for 0% of the time, Pallas kernels for 0%

profile of v1, /device:TPU:1, one launch (start us, length us, event | category | flops | bytes accessed | tf_op | source)
XLA Modules:
  0.0 374.7 jit_solution(11524459674680655166)
XLA Ops:
  6.5 0.0 copy-start
  6.5 0.0 copy-start.3
  6.5 0.0 copy-start.9
  6.5 0.0 copy-start.8
  6.5 0.0 reduce-scatter.3.cloned.1.call-start
  6.6 0.0 copy-start.1
  6.6 10.7 %convert_reduce_fusion = f32[256,64]{0,1:T(8,128)S(1)} fusion(bf16[256,64,128]{2,1,0:T(8,128)(2,1)} %param.12), kind=kLoop, calls=%fused_computation.2 | loop fusion | flops 4177920 | bytes 4259840 | tf_op jit(solution)/shard_map/reduce_sum | solution.py:26
  17.3 0.0 copy-done.1
  17.3 11.6 %fusion.2 = f32[256,64]{0,1:T(8,128)S(1)} fusion(f32[256,64]{0,1:T(8,128)S(1)} %broadcast_multiply_fusion, bf16[256,64,128]{2,1,0:T(8,128)(2,1)S(1)} %copy-done.1), kind=kLoop, calls=%fused_computation.5 | loop fusion | flops 8372224 | bytes 4325376 | tf_op jit(solution)/shard_map/reduce_sum | solution.py:28
  29.0 0.0 copy-done.3
  29.0 0.0 copy-done.9
  29.0 0.0 copy-done.8
  29.0 0.0 copy-start.4
  29.0 0.0 copy-start.5
  29.0 0.0 copy-start.6
  29.1 0.0 copy-start.7
  29.1 9.3 %fusion.5 = bf16[256,64,128]{2,0,1:T(8,128)(2,1)S(1)} fusion(f32[128]{0:T(128)S(1)} %copy-done.8, f32[128]{0:T(128)S(1)} %copy-done.9, f32[256,64]{0,1:T(8,128)S(1)} %add_rsqrt_fusion.1, f32[256,64]{0,1:T(8,128)S(1)} %broadcast_multiply_fusion, bf16[256,64,128]{2,1,0:T(8,128)(2,1)S(1)} %copy-done.1), kind=kLoop, calls=%fused_computation.8 | loop fusion | flops 12582912 | bytes 8520704 | tf_op jit(solution)/shard_map/convert_element_type | solution.py:29
  38.4 0.0 copy-done.4
  38.4 0.0 copy-done.5
  38.4 0.0 copy-done.6
  38.4 0.0 copy-done.7
  38.4 0.0 copy-start.2
  38.4 1.3 fusion.25
  39.7 0.7 copy-done.2
  40.3 1.4 fusion.12
  41.8 0.6 copy.19
  42.4 0.5 stack.2
  42.9 52.9 %all_to_all.5 = bf16[4,32,256,64]{2,3,1,0:T(8,128)(2,1)S(1)} all-to-all(bf16[4,32,256,64]{2,3,1,0:T(8,128)(2,1)S(1)} %stack.2), channel_id=1, replica_groups=mesh['row'=4,'col'=16,'chan'=4] {'row'}, dimensions={0} | all-to-all | bytes 8388608 | tf_op jit(solution)/shard_map/all_to_all | solution.py:48
  95.8 0.5 copy.24
  96.3 8.2 %convert_bitcast_fusion = bf16[1024,32,256]{2,0,1:T(8,128)(2,1)} fusion(bf16[32,1024,64]{1,2,0:T(8,128)(2,1)S(1)} %bitcast.20, bf16[32,256,64]{1,0,2:T(8,128)(2,1)S(1)} %get-tuple-element.7), kind=kOutput, calls=%fused_computation | convolution fusion | flops 1082130432 | bytes 22020096 | tf_op jit(solution)/shard_map/hik,hjk->jhi/dot_general | solution.py:51
  104.5 0.0 copy-start.11
  104.5 0.0 copy-start.12
  104.5 0.0 reduce-scatter.3.cloned.1.call-update
  104.5 0.0 all-reduce.3.cloned.1.call-start
  104.6 117.0 %reduce-scatter.3.cloned.1.call-done = bf16[64,32,256]{2,0,1:T(8,128)(2,1)} async-done(((bf16[1024,32,256]{2,0,1:T(8,128)(2,1)}), bf16[64,32,256]{2,0,1:T(8,128)(2,1)}) %reduce-scatter.3.cloned.1.call-update) | async-done | bytes 1048592 | tf_op jit(solution)/shard_map/reduce_scatter | solution.py:50
  221.6 2.1 fusion.10
  223.7 2.0 reduce_sum.41
  225.7 0.0 all-reduce.3.cloned.1.call-update
  225.7 0.3 reduce-scatter.5.cloned.1.call-start
  226.0 0.0 copy-done.11
  226.0 0.1 dynamic_slice.13
  226.0 0.0 copy-done.12
  226.0 0.1 dynamic_slice.14
  226.1 47.1 %all-reduce.3.cloned.1.call-done = (bf16[64,256]{1,0:T(8,128)(2,1)}, bf16[64,256]{1,0:T(8,128)(2,1)}) async-done(((bf16[64,256]{1,0:T(8,128)(2,1)}, bf16[64,256]{1,0:T(8,128)(2,1)}), (bf16[64,256]{1,0:T(8,128)(2,1)}, bf16[64,256]{1,0:T(8,128)(2,1)})) %all-reduce.3.cloned.1.call-update) | async-done | bytes 65552 | tf_op jit(solution)/shard_map/psum | solution.py:64
  273.2 0.8 convert_multiply_fusion.1
  274.0 1.6 fusion.9
  275.7 0.0 copy-done
  275.7 0.0 copy-start.10
  275.7 3.3 convolution_convert_fusion
  279.0 0.0 reduce-scatter.5.cloned.1.call-update
  279.0 85.3 %reduce-scatter.5.cloned.1.call-done = bf16[16,256,128]{2,1,0:T(8,128)(2,1)} async-done(((bf16[64,256,128]{2,1,0:T(8,128)(2,1)}), bf16[16,256,128]{2,1,0:T(8,128)(2,1)}) %reduce-scatter.5.cloned.1.call-update) | async-done | bytes 1048592 | tf_op jit(solution)/shard_map/reduce_scatter | solution.py:78
  364.3 0.0 copy-done.10
  364.3 2.2 fusion.21
  366.5 1.6 copy.23
  (3 shorter events, 0.0 us)
Async XLA Ops:
  6.5 269.1 %copy-start = (bf16[128,128]{1,0:T(8,128)(2,1)S(1)}, bf16[128,128]{1,0:T(8,128)(2,1)}, u32[]{:S(2)}) copy-start(bf16[128,128]{1,0:T(8,128)(2,1)} %param.22) | copy-start | bytes 98308
  6.5 22.4 %copy-start.3 = (s32[256,64]{0,1:T(8,128)S(1)}, s32[256,64]{0,1:T(8,128)}, u32[]{:S(2)}) copy-start(s32[256,64]{0,1:T(8,128)} %param.13) | copy-start | bytes 196612
  6.5 22.5 %copy-start.9 = (f32[128]{0:T(128)S(1)}, f32[128]{0:T(128)}, u32[]{:S(2)}) copy-start(f32[128]{0:T(128)} %param.14) | copy-start | bytes 1540
  6.5 22.5 %copy-start.8 = (f32[128]{0:T(128)S(1)}, f32[128]{0:T(128)}, u32[]{:S(2)}) copy-start(f32[128]{0:T(128)} %param.15) | copy-start | bytes 1540
  6.5 215.1 %reduce-scatter.3.cloned.1.call-start = ((), (), s32[]{:S(2)}) async-start(), calls=%async_computation.3 | async-start | bytes 17825792 | tf_op jit(solution)/shard_map/reduce_scatter | solution.py:50
  6.6 10.7 %copy-start.1 = (bf16[256,64,128]{2,1,0:T(8,128)(2,1)S(1)}, bf16[256,64,128]{2,1,0:T(8,128)(2,1)}, u32[]{:S(2)}) copy-start(bf16[256,64,128]{2,1,0:T(8,128)(2,1)} %param.12) | copy-start | bytes 12582916
  29.0 9.3 %copy-start.4 = (bf16[128,32]{0,1:T(8,128)(2,1)S(1)}, bf16[128,32]{0,1:T(8,128)(2,1)}, u32[]{:S(2)}) copy-start(bf16[128,32]{0,1:T(8,128)(2,1)} %param.19) | copy-start | bytes 24580
  29.0 9.3 %copy-start.5 = (bf16[128,32]{0,1:T(8,128)(2,1)S(1)}, bf16[128,32]{0,1:T(8,128)(2,1)}, u32[]{:S(2)}) copy-start(bf16[128,32]{0,1:T(8,128)(2,1)} %param.18) | copy-start | bytes 24580
  29.0 9.3 %copy-start.6 = (bf16[128,32]{0,1:T(8,128)(2,1)S(1)}, bf16[128,32]{0,1:T(8,128)(2,1)}, u32[]{:S(2)}) copy-start(bf16[128,32]{0,1:T(8,128)(2,1)} %param.17) | copy-start | bytes 24580
  29.1 9.3 %copy-start.7 = (bf16[128,32]{0,1:T(8,128)(2,1)S(1)}, bf16[128,32]{0,1:T(8,128)(2,1)}, u32[]{:S(2)}) copy-start(bf16[128,32]{0,1:T(8,128)(2,1)} %param.16) | copy-start | bytes 24580
  38.4 1.9 copy-start.2
  104.5 121.5 %copy-start.11 = (f32[128]{0:T(128)S(1)}, f32[128]{0:T(128)}, u32[]{:S(2)}) copy-start(f32[128]{0:T(128)} %param.20) | copy-start | bytes 1540
  104.5 121.5 %copy-start.12 = (f32[128]{0:T(128)S(1)}, f32[128]{0:T(128)}, u32[]{:S(2)}) copy-start(f32[128]{0:T(128)} %param.21) | copy-start | bytes 1540
  104.5 168.7 %all-reduce.3.cloned.1.call-start = ((), (), s32[]{:S(2)}) async-start(), calls=%async_computation.5 | async-start | bytes 131072 | tf_op jit(solution)/shard_map/psum | solution.py:64
  225.7 138.6 %reduce-scatter.5.cloned.1.call-start = ((), (), s32[]{:S(2)}) async-start(), calls=%async_computation.4 | async-start | bytes 5242880 | tf_op jit(solution)/shard_map/reduce_scatter | solution.py:78
  275.7 88.6 %copy-start.10 = (bf16[128,128]{1,0:T(8,128)(2,1)S(1)}, bf16[128,128]{1,0:T(8,128)(2,1)}, u32[]{:S(2)}) copy-start(bf16[128,128]{1,0:T(8,128)(2,1)} %param.23) | copy-start | bytes 98308
Sparse Core Ops, SparseCore 0:
  104.7 116.8 reduce-scatter.2
  225.8 47.3 all-reduce.2
  279.1 85.1 reduce-scatter.4
